TPU v7x, 512 devices: a whole 4x4x16 slice. The times are simulated.
512 devices in a mesh: group: 32 (over z_lo, x), fsdp: 16 (over y, z_hi, core).
Axes of the slice: x: 4, y: 4, z: 16 (z_hi: 2, z_lo: 8; z = z_hi * 8 + z_lo), core: 2. Of those that a mesh axis runs over, the one named last changes fastest.
Arguments:
- tokens: bfloat16 [32, 2048, 2304], P('group', 'fsdp'), may hold values from -6 to 6
- token_ids: int32 [32, 2048], P('group', 'fsdp'), may hold values from 0 to 255999
- weight: bfloat16 [32, 2304, 1024], P('group', 'fsdp'), may hold values from -0.125 to 0.125
- stale_weight: bfloat16 [32, 2304, 1024], P('group', 'fsdp'), may hold values from -0.125 to 0.125
- gain: bfloat16 [32, 2304], P('group'), may hold values from 0.099609375 to 1.8984375
- stale_gain: bfloat16 [32, 2304], P('group'), may hold values from 0.099609375 to 1.8984375
- partner: int32 [32], replicated, may hold values from 0 to 31, as said below
Outputs:
- grad_weight: float32 [32, 2304, 1024], P('group', 'fsdp')
- grad_tokens: bfloat16 [32, 2048, 2304], P('group', 'fsdp')
- token_loss: float32 [32, 2048], P('group', 'fsdp')
Inputs may be any that keep to these rules, and one draw needn't show every extreme that they name: partner[g] = g XOR m for one m of 1 to 31, the same for all g.
All inputs are finite; a program needn't handle non-finite values.
Results may differ from a plain program's by a relative error of at most 0.01.
Values may be sent and summed in bfloat16 or wider, within the bound.
A program may use at most 64 MiB of HBM per device.

v0:
```python
import jax
import jax.numpy as jnp
from jax import lax
from jax.sharding import PartitionSpec as P


def partner_2(array, axis, apart):
    return lax.ppermute(array, axis, [(i, i ^ 1 << apart) for i in range(lax.axis_size(axis))])


def swap_pair(pair, bit):
    return partner_2((pair[0], pair[1]), "group", bit)


def body(tokens, token_ids, weight, stale_weight, gain, stale_gain, partner):
    x = tokens[0].astype(jnp.float32)
    rstd = lax.rsqrt(jnp.mean(x * x, axis=-1, keepdims=True) + 1e-06)
    normed = x * rstd
    gain_now = gain[0].astype(jnp.float32)
    student_in = (normed * gain_now).astype(jnp.bfloat16)
    flip = partner[0]
    teacher_w = stale_weight[0]
    teacher_g = stale_gain[0]
    nbits = lax.axis_size("group").bit_length() - 1
    for bit in range(nbits):
        taken = jnp.bitwise_and(jnp.right_shift(flip, bit), 1) == 1
        got_w, got_g = swap_pair((teacher_w, teacher_g), bit)
        teacher_w = jnp.where(taken, got_w, teacher_w)
        teacher_g = jnp.where(taken, got_g, teacher_g)
    teacher_in = (normed * teacher_g.astype(jnp.float32)).astype(jnp.bfloat16)
    tok_rows = x.shape[0]
    chans = teacher_in
    teacher_out = jnp.dot(
        chans,
        lax.all_gather(teacher_w, "fsdp", axis=0, tiled=True),
        preferred_element_type=jnp.float32,
    )
    full_rows = lax.all_gather(weight[0], "fsdp", axis=0, tiled=True)
    student_out = jnp.dot(student_in, full_rows, preferred_element_type=jnp.float32)
    keep = (token_ids[0] != 0).astype(jnp.float32)[:, None]
    diff = keep * (student_out - teacher_out)
    token_loss = 0.5 * jnp.mean(diff * diff, axis=-1)
    out_grad = diff.astype(jnp.bfloat16)
    columns = lax.all_to_all(student_in, "fsdp", split_axis=1, concat_axis=0, tiled=True)
    chans = columns
    grad_w = lax.dot_general(
        chans,
        lax.all_gather(out_grad, "fsdp", axis=0, tiled=True),
        (((0,), (0,)), ((), ())),
        preferred_element_type=jnp.float32,
    )
    group_tokens = tok_rows * lax.axis_size("fsdp")
    grad_w = grad_w / jnp.sqrt(jnp.float32(group_tokens))
    in_grad = lax.dot_general(
        out_grad, full_rows, (((1,), (1,)), ((), ())), preferred_element_type=jnp.float32
    )
    scaled = in_grad * gain_now
    grad_x = rstd * (scaled - normed * jnp.mean(scaled * normed, axis=-1, keepdims=True))
    return (grad_w[None], grad_x.astype(jnp.bfloat16)[None], token_loss[None])


def solution(mesh):
    return jax.shard_map(
        body,
        mesh=mesh,
        in_specs=(
            P("group", "fsdp", None),
            P("group", "fsdp"),
            P("group", "fsdp", None),
            P("group", "fsdp", None),
            P("group", None),
            P("group", None),
            P(),
        ),
        out_specs=(P("group", "fsdp", None), P("group", "fsdp", None), P("group", "fsdp")),
        check_vma=False,
    )
```

profile of v0, /device:TPU:1, one launch (start us, length us, event | category | flops | bytes accessed | tf_op | source)
XLA Modules:
  0.0 432.7 jit_solution(14007763068484107217)
XLA Ops:
  7.2 0.0 copy-start.4
  7.2 0.0 all-gather.9.cloned.1.call-start
  7.2 0.7 all-gather.9.cloned.1.call-update
  7.9 0.0 all-gather.5.cloned.1.call-start
  8.0 3.9 collective-permute-start.5
  12.6 3.7 collective-permute-done.5
  16.2 1.0 broadcast_select_fusion
  17.2 7.2 %collective-permute-start.6 = (bf16[144,1024]{1,0:T(8,128)(2,1)S(1)}, bf16[144,1024]{1,0:T(8,128)(2,1)S(1)}, u32[]{:S(2)}, u32[]{:S(2)}) collective-permute-start(bf16[144,1024]{1,0:T(8,128)(2,1)S(1)} %broadcast_select_fusion), channel_id=1, source_target_pairs={{0,32},{16,48},{32,0},{48,16},{64,96},{80,112},{96,64},{112,80},{1... | collective-permute-start | bytes 884744 | tf_op jit(solution)/shard_map/ppermute | solution.py:8
  24.4 0.0 copy-done.4
  24.5 4.3 %collective-permute-done.6 = bf16[144,1024]{1,0:T(8,128)(2,1)S(1)} collective-permute-done((bf16[144,1024]{1,0:T(8,128)(2,1)S(1)}, bf16[144,1024]{1,0:T(8,128)(2,1)S(1)}, u32[]{:S(2)}, u32[]{:S(2)}) %collective-permute-start.6) | collective-permute-done | bytes 294944 | tf_op jit(solution)/shard_map/ppermute | solution.py:8
  28.9 4.8 %collective-permute-start.7 = (bf16[144,1024]{1,0:T(8,128)(2,1)S(1)}, bf16[144,1024]{1,0:T(8,128)(2,1)S(1)}, u32[]{:S(2)}, u32[]{:S(2)}) collective-permute-start(bf16[144,1024]{1,0:T(8,128)(2,1)S(1)} %broadcast_select_fusion.1), channel_id=1, source_target_pairs={{0,64},{16,80},{32,96},{48,112},{64,0},{80,16},{96,32},{112,48},{1... | collective-permute-start | bytes 884744 | tf_op jit(solution)/shard_map/ppermute | solution.py:8
  33.7 15.0 %collective-permute-done.7 = bf16[144,1024]{1,0:T(8,128)(2,1)S(1)} collective-permute-done((bf16[144,1024]{1,0:T(8,128)(2,1)S(1)}, bf16[144,1024]{1,0:T(8,128)(2,1)S(1)}, u32[]{:S(2)}, u32[]{:S(2)}) %collective-permute-start.7) | collective-permute-done | bytes 294944 | tf_op jit(solution)/shard_map/ppermute | solution.py:8
  48.8 0.0 copy-start.2
  48.8 0.0 copy-start
  48.8 8.8 %collective-permute-start.8 = (bf16[144,1024]{1,0:T(8,128)(2,1)S(1)}, bf16[144,1024]{1,0:T(8,128)(2,1)S(1)}, u32[]{:S(2)}, u32[]{:S(2)}) collective-permute-start(bf16[144,1024]{1,0:T(8,128)(2,1)S(1)} %broadcast_select_fusion.2), channel_id=1, source_target_pairs={{0,128},{16,144},{32,160},{48,176},{64,192},{80,208},{96,224},{112... | collective-permute-start | bytes 884744 | tf_op jit(solution)/shard_map/ppermute | solution.py:8
  57.6 12.5 %collective-permute-done.8 = bf16[144,1024]{1,0:T(8,128)(2,1)S(1)} collective-permute-done((bf16[144,1024]{1,0:T(8,128)(2,1)S(1)}, bf16[144,1024]{1,0:T(8,128)(2,1)S(1)}, u32[]{:S(2)}, u32[]{:S(2)}) %collective-permute-start.8) | collective-permute-done | bytes 294944 | tf_op jit(solution)/shard_map/ppermute | solution.py:8
  70.1 7.3 %collective-permute-start.9 = (bf16[144,1024]{1,0:T(8,128)(2,1)S(1)}, bf16[144,1024]{1,0:T(8,128)(2,1)S(1)}, u32[]{:S(2)}, u32[]{:S(2)}) collective-permute-start(bf16[144,1024]{1,0:T(8,128)(2,1)S(1)} %broadcast_select_fusion.3), channel_id=1, source_target_pairs={{0,256},{16,272},{32,288},{48,304},{64,320},{80,336},{96,352},{112... | collective-permute-start | bytes 884744 | tf_op jit(solution)/shard_map/ppermute | solution.py:8
  77.5 76.0 %collective-permute-done.9 = bf16[144,1024]{1,0:T(8,128)(2,1)S(1)} collective-permute-done((bf16[144,1024]{1,0:T(8,128)(2,1)S(1)}, bf16[144,1024]{1,0:T(8,128)(2,1)S(1)}, u32[]{:S(2)}, u32[]{:S(2)}) %collective-permute-start.9) | collective-permute-done | bytes 294944 | tf_op jit(solution)/shard_map/ppermute | solution.py:8
  153.4 0.7 broadcast_select_fusion.4
  154.2 0.0 all-gather.5.cloned.1.call-update
  154.2 0.0 all-gather.7.cloned.1.call-start
  154.2 0.0 copy-done.2
  154.3 3.3 collective-permute-start
  157.6 1.1 collective-permute-done
  158.7 5.0 %collective-permute-start.1 = (bf16[2304]{0:T(1024)(128)(2,1)S(1)}, bf16[2304]{0:T(1024)(128)(2,1)S(1)}, u32[]{:S(2)}, u32[]{:S(2)}) collective-permute-start(bf16[2304]{0:T(1024)(128)(2,1)S(1)} %broadcast_select_fusion.5), channel_id=1, source_target_pairs={{0,32},{16,48},{32,0},{48,16},{64,96},{80,112},{96,64},{112,80},{1... | collective-permute-start | bytes 13832 | tf_op jit(solution)/shard_map/ppermute | solution.py:8
  163.7 0.2 fusion.9
  163.9 0.8 collective-permute-done.1
  164.7 1.9 collective-permute-start.2
  166.6 2.4 collective-permute-done.2
  169.1 1.9 collective-permute-start.3
  171.0 3.3 collective-permute-done.3
  174.4 4.6 %collective-permute-start.4 = (bf16[2304]{0:T(1024)(128)(2,1)S(1)}, bf16[2304]{0:T(1024)(128)(2,1)S(1)}, u32[]{:S(2)}, u32[]{:S(2)}) collective-permute-start(bf16[2304]{0:T(1024)(128)(2,1)S(1)} %broadcast_select_fusion.8), channel_id=1, source_target_pairs={{0,256},{16,272},{32,288},{48,304},{64,320},{80,336},{96,352},{112... | collective-permute-start | bytes 13832 | tf_op jit(solution)/shard_map/ppermute | solution.py:8
  179.0 3.8 collective-permute-done.4
  182.7 3.2 fusion.2
  185.9 103.1 %all-gather.5.cloned.1.call-done = bf16[2304,1024]{1,0:T(8,128)(2,1)} async-done(((bf16[144,1024]{1,0:T(8,128)(2,1)}), bf16[2304,1024]{1,0:T(8,128)(2,1)}) %all-gather.5.cloned.1.call-update) | async-done | bytes 4718608 | tf_op jit(solution)/shard_map/all_gather | solution.py:35
  289.0 3.9 multiply_reduce_fusion.1
  292.9 0.0 all-gather.7.cloned.1.call-update
  292.9 0.1 mul.94
  293.0 0.2 copy.10
  293.2 0.0 copy-start.1
  293.2 1.2 multiply_convert_fusion.3
  294.4 3.9 all-to-all-start
  298.3 4.1 multiply_reduce_fusion
  302.5 0.5 multiply_bitcast_fusion
  303.0 1.2 fusion.10
  304.2 20.7 %all-to-all-done = bf16[128,16,144]{0,2,1:T(8,128)(2,1)S(1)} async-done(((bf16[128,16,144]{0,2,1:T(8,128)(2,1)}), bf16[128,16,144]{0,2,1:T(8,128)(2,1)S(1)}, u32[]{:S(2)}, u32[]{:S(2)}) %all-to-all-start) | async-done | bytes 589856 | tf_op jit(solution)/shard_map/all_to_all | solution.py:44
  324.9 97.5 %all-gather.7.cloned.1.call-done = bf16[2048,1024]{1,0:T(8,128)(2,1)} async-done(((bf16[128,1024]{1,0:T(8,128)(2,1)}), bf16[2048,1024]{1,0:T(8,128)(2,1)}) %all-gather.7.cloned.1.call-update) | async-done | bytes 4194320 | tf_op jit(solution)/shard_map/all_gather | solution.py:48
  422.4 3.8 fusion.7
  (20 shorter events, 0.2 us)
Async XLA Ops:
  7.2 17.3 %copy-start.4 = (s32[32]{0:T(128)S(1)}, s32[32]{0:T(128)}, u32[]{:S(2)}) copy-start(s32[32]{0:T(128)} %param.13) | copy-start | bytes 388
  7.2 175.6 %all-gather.9.cloned.1.call-start = ((), (), s32[]{:S(2)}) async-start(), calls=%async_computation.3 | async-start | bytes 5013504 | tf_op jit(solution)/shard_map/all_gather | solution.py:38
  7.9 281.1 %all-gather.5.cloned.1.call-start = ((), (), s32[]{:S(2)}) async-start(), calls=%async_computation.1 | async-start | bytes 5013504 | tf_op jit(solution)/shard_map/all_gather | solution.py:35
  8.0 8.3 %collective-permute-start.5 = (bf16[144,1024]{1,0:T(8,128)(2,1)}, bf16[144,1024]{1,0:T(8,128)(2,1)S(1)}, u32[]{:S(2)}, u32[]{:S(2)}) collective-permute-start(bf16[144,1024]{1,0:T(8,128)(2,1)} %bitcast.57), channel_id=1, source_target_pairs={{0,16},{16,0},{32,48},{48,32},{64,80},{80,64},{96,112},{112,96},{1... | collective-permute-start | bytes 884744 | tf_op jit(solution)/shard_map/ppermute | solution.py:8
  17.2 11.6 %collective-permute-start.6 = (bf16[144,1024]{1,0:T(8,128)(2,1)S(1)}, bf16[144,1024]{1,0:T(8,128)(2,1)S(1)}, u32[]{:S(2)}, u32[]{:S(2)}) collective-permute-start(bf16[144,1024]{1,0:T(8,128)(2,1)S(1)} %broadcast_select_fusion), channel_id=1, source_target_pairs={{0,32},{16,48},{32,0},{48,16},{64,96},{80,112},{96,64},{112,80},{1... | collective-permute-start | bytes 884744 | tf_op jit(solution)/shard_map/ppermute | solution.py:8
  28.9 19.9 %collective-permute-start.7 = (bf16[144,1024]{1,0:T(8,128)(2,1)S(1)}, bf16[144,1024]{1,0:T(8,128)(2,1)S(1)}, u32[]{:S(2)}, u32[]{:S(2)}) collective-permute-start(bf16[144,1024]{1,0:T(8,128)(2,1)S(1)} %broadcast_select_fusion.1), channel_id=1, source_target_pairs={{0,64},{16,80},{32,96},{48,112},{64,0},{80,16},{96,32},{112,48},{1... | collective-permute-start | bytes 884744 | tf_op jit(solution)/shard_map/ppermute | solution.py:8
  48.8 105.5 %copy-start.2 = (bf16[1,2304]{1,0:T(2,128)(2,1)S(1)}, bf16[1,2304]{1,0:T(2,128)(2,1)}, u32[]{:S(2)}) copy-start(bf16[1,2304]{1,0:T(2,128)(2,1)} %param.12) | copy-start | bytes 13828
  48.8 114.9 %copy-start = (bf16[1,128,2304]{2,1,0:T(8,128)(2,1)S(1)}, bf16[1,128,2304]{2,1,0:T(8,128)(2,1)}, u32[]{:S(2)}) copy-start(bf16[1,128,2304]{2,1,0:T(8,128)(2,1)} %param.7) | copy-start | bytes 1769476
  48.8 21.3 %collective-permute-start.8 = (bf16[144,1024]{1,0:T(8,128)(2,1)S(1)}, bf16[144,1024]{1,0:T(8,128)(2,1)S(1)}, u32[]{:S(2)}, u32[]{:S(2)}) collective-permute-start(bf16[144,1024]{1,0:T(8,128)(2,1)S(1)} %broadcast_select_fusion.2), channel_id=1, source_target_pairs={{0,128},{16,144},{32,160},{48,176},{64,192},{80,208},{96,224},{112... | collective-permute-start | bytes 884744 | tf_op jit(solution)/shard_map/ppermute | solution.py:8
  70.1 100.9 %copy-start.5 = (s32[1,128]{1,0:T(1,128)S(1)}, s32[1,128]{1,0:T(1,128)}, u32[]{:S(2)}) copy-start(s32[1,128]{1,0:T(1,128)} %param.8) | copy-start | bytes 1540
  70.1 108.8 %copy-start.3 = (bf16[1,2304]{1,0:T(2,128)(2,1)S(1)}, bf16[1,2304]{1,0:T(2,128)(2,1)}, u32[]{:S(2)}) copy-start(bf16[1,2304]{1,0:T(2,128)(2,1)} %param.11) | copy-start | bytes 13828
  70.1 83.3 %collective-permute-start.9 = (bf16[144,1024]{1,0:T(8,128)(2,1)S(1)}, bf16[144,1024]{1,0:T(8,128)(2,1)S(1)}, u32[]{:S(2)}, u32[]{:S(2)}) collective-permute-start(bf16[144,1024]{1,0:T(8,128)(2,1)S(1)} %broadcast_select_fusion.3), channel_id=1, source_target_pairs={{0,256},{16,272},{32,288},{48,304},{64,320},{80,336},{96,352},{112... | collective-permute-start | bytes 884744 | tf_op jit(solution)/shard_map/ppermute | solution.py:8
  154.2 268.2 %all-gather.7.cloned.1.call-start = ((), (), s32[]{:S(2)}) async-start(), calls=%async_computation.2 | async-start | bytes 4456448 | tf_op jit(solution)/shard_map/all_gather | solution.py:48
  154.3 4.4 %collective-permute-start = (bf16[2304]{0:T(1024)(128)(2,1)S(1)}, bf16[2304]{0:T(1024)(128)(2,1)S(1)}, u32[]{:S(2)}, u32[]{:S(2)}) collective-permute-start(bf16[2304]{0:T(1024)(128)(2,1)S(1)} %reduce.2), channel_id=1, source_target_pairs={{0,16},{16,0},{32,48},{48,32},{64,80},{80,64},{96,112},{112,96},{1... | collective-permute-start | bytes 13832 | tf_op jit(solution)/shard_map/ppermute | solution.py:8
  158.7 6.0 %collective-permute-start.1 = (bf16[2304]{0:T(1024)(128)(2,1)S(1)}, bf16[2304]{0:T(1024)(128)(2,1)S(1)}, u32[]{:S(2)}, u32[]{:S(2)}) collective-permute-start(bf16[2304]{0:T(1024)(128)(2,1)S(1)} %broadcast_select_fusion.5), channel_id=1, source_target_pairs={{0,32},{16,48},{32,0},{48,16},{64,96},{80,112},{96,64},{112,80},{1... | collective-permute-start | bytes 13832 | tf_op jit(solution)/shard_map/ppermute | solution.py:8
  164.7 4.4 %collective-permute-start.2 = (bf16[2304]{0:T(1024)(128)(2,1)S(1)}, bf16[2304]{0:T(1024)(128)(2,1)S(1)}, u32[]{:S(2)}, u32[]{:S(2)}) collective-permute-start(bf16[2304]{0:T(1024)(128)(2,1)S(1)} %broadcast_select_fusion.6), channel_id=1, source_target_pairs={{0,64},{16,80},{32,96},{48,112},{64,0},{80,16},{96,32},{112,48},{1... | collective-permute-start | bytes 13832 | tf_op jit(solution)/shard_map/ppermute | solution.py:8
  169.1 5.3 %collective-permute-start.3 = (bf16[2304]{0:T(1024)(128)(2,1)S(1)}, bf16[2304]{0:T(1024)(128)(2,1)S(1)}, u32[]{:S(2)}, u32[]{:S(2)}) collective-permute-start(bf16[2304]{0:T(1024)(128)(2,1)S(1)} %broadcast_select_fusion.7), channel_id=1, source_target_pairs={{0,128},{16,144},{32,160},{48,176},{64,192},{80,208},{96,224},{112... | collective-permute-start | bytes 13832 | tf_op jit(solution)/shard_map/ppermute | solution.py:8
  174.4 8.4 %collective-permute-start.4 = (bf16[2304]{0:T(1024)(128)(2,1)S(1)}, bf16[2304]{0:T(1024)(128)(2,1)S(1)}, u32[]{:S(2)}, u32[]{:S(2)}) collective-permute-start(bf16[2304]{0:T(1024)(128)(2,1)S(1)} %broadcast_select_fusion.8), channel_id=1, source_target_pairs={{0,256},{16,272},{32,288},{48,304},{64,320},{80,336},{96,352},{112... | collective-permute-start | bytes 13832 | tf_op jit(solution)/shard_map/ppermute | solution.py:8
  293.2 5.1 %copy-start.1 = (bf16[128,1024]{1,0:T(8,128)(2,1)S(1)}, bf16[128,1024]{1,0:T(8,128)(2,1)}, u32[]{:S(2)}) copy-start(bf16[128,1024]{1,0:T(8,128)(2,1)} %get-tuple-element.4) | copy-start | bytes 786436
  294.4 30.5 %all-to-all-start = ((bf16[128,16,144]{0,2,1:T(8,128)(2,1)}), bf16[128,16,144]{0,2,1:T(8,128)(2,1)S(1)}, u32[]{:S(2)}, u32[]{:S(2)}) async-start(bf16[128,16,144]{0,2,1:T(8,128)(2,1)} %multiply_convert_fusion.3), calls=%async_computation | async-start | bytes 1179648 | tf_op jit(solution)/shard_map/all_to_all | solution.py:44
Sparse Core Ops, SparseCore 0:
  11.3 129.6 all-gather.8
  154.3 134.6 all-gather.4
  293.0 129.3 all-gather.6
where the time goes:
time: 433 us
  waiting for transfers between devices  345 us (80%)
  starting transfers between devices  52.8 us (12%)
  matrix products  15 us (3%)
  between operations  14.8 us (3%)
  other arithmetic  5.03 us (1%)
    ppermute x10, waiting for transfers between devices, partner_2(): lax.ppermute(array, axis, [(i, i ^ 1 << apart) for i in range(lax.axis_si...  123 us
    all_gather x1, waiting for transfers between devices, body(): lax.all_gather(teacher_w, 'fsdp', axis=0, tiled=True)  103 us
    all_gather x1, waiting for transfers between devices, body(): lax.all_gather(out_grad, 'fsdp', axis=0, tiled=True)  97.5 us
    ppermute x10, starting transfers between devices, partner_2(): lax.ppermute(array, axis, [(i, i ^ 1 << apart) for i in range(lax.axis_si...  48.7 us
    all_to_all x1, waiting for transfers between devices, body(): lax.all_to_all(student_in, 'fsdp', split_axis=1, concat_axis=0, tiled=True)  20.7 us
  transfers between devices with their start and end apart: 14, of which 13 were waited for; matrix products, arithmetic and copies ran while one was open for 3% of the time, Pallas kernels for 0%

commit v1 on v0

v1 whole, which is shorter than its diff:
```python
import functools

import jax
import jax.numpy as jnp
from jax import lax
from jax.experimental import pallas as pl
from jax.experimental.pallas import tpu as pltpu
from jax.sharding import PartitionSpec as P

MESH = pl.DeviceIdType.MESH
NY = 4
CHUNKS = 4
F32 = jnp.float32
BF16 = jnp.bfloat16


def step_kernel(
    x_ref, keep_ref, w_ref, sa_ref, sb_ref, gain_ref, sgain_ref,
    gw_ref, gt_ref, loss_ref,
    x4, xc, xt, wfull, sfull, gcol, sgcol, grow,
    pself, psend, precv, og, igacc, igsend, igrecv,
    gmsend, gmrecv, gzkeep, gzsend, gzrecv, rstd_ref,
    ysend, yrecv, csend, crecv, zsend, zrecv,
):
    tok, dim = x_ref.shape
    rows, feat = w_ref.shape
    chans = dim // NY
    width = feat // CHUNKS
    grp = lax.axis_index("group")
    me = lax.axis_index("fsdp")
    y = me // 4
    zc = lax.rem(me, 4)
    zh = zc // 2
    core = lax.rem(zc, 2)
    mate = (grp, y * 4 + zh * 2 + (1 - core))
    twin = (grp, y * 4 + (1 - zh) * 2 + core)

    def at_y(k):
        return (grp, lax.rem(y + k, NY) * 4 + zc)

    def remote(src, dst, ss, rs, dev):
        return pltpu.make_async_remote_copy(
            src_ref=src, dst_ref=dst, send_sem=ss, recv_sem=rs,
            device_id=dev, device_id_type=MESH,
        )

    def block(b):
        return pl.ds(pl.multiple_of(b * rows, 16), rows)

    sent = []

    def go(copy):
        copy.start()
        sent.append(copy)

    barrier = pltpu.get_barrier_semaphore()
    for peer in [mate, twin] + [at_y(k) for k in range(1, NY)]:
        pl.semaphore_signal(barrier, inc=1, device_id=peer, device_id_type=MESH)

    for q in range(NY):
        x4[q] = x_ref[:, q * chans:(q + 1) * chans]
    mine = zc
    wfull[block(mine), :] = w_ref[...]
    pl.semaphore_wait(barrier, NY + 1)

    cols = [pl.ds(f * width, width) for f in range(CHUNKS)]
    for f in range(CHUNKS):
        go(remote(w_ref.at[:, cols[f]], wfull.at[block(mine), cols[f]],
                  zsend.at[f], zrecv.at[f], twin))
    far = (1 - zh) * 2 + core
    go(remote(w_ref, wfull.at[block(mine), :], csend.at[0], crecv.at[0], mate))
    go(remote(sa_ref, sfull.at[block(mine), :], csend.at[1], crecv.at[1], mate))
    go(remote(sb_ref, sfull.at[block(far), :], csend.at[2], crecv.at[2], mate))
    for k in range(1, NY):
        go(remote(x4.at[lax.rem(y + k, NY)], xc.at[k], ysend.at[0, k], yrecv.at[0, k], at_y(k)))
    xc[0] = x4[y]
    sfull[block(mine), :] = sa_ref[...]
    sfull[block(far), :] = sb_ref[...]

    xf = x_ref[...].astype(F32)
    rstd_ref[...] = lax.rsqrt(jnp.mean(xf * xf, axis=1, keepdims=True) + 1e-06)
    for q in range(NY):
        grow[q] = gain_ref[:, q * chans:(q + 1) * chans].astype(F32)

    gcol[...] = jnp.broadcast_to(grow[y], (128, chans)).T
    sgcol[...] = jnp.broadcast_to(sgain_ref[...].astype(F32), (128, chans)).T

    def y_wait(n, k, ref):
        remote(ref, ref, ysend.at[n, k], yrecv.at[n, k], at_y(k)).wait_recv()

    def c_wait(n, ref):
        remote(ref, ref, csend.at[n], crecv.at[n], mate).wait_recv()

    def z_wait(n, ref):
        remote(ref, ref, zsend.at[n], zrecv.at[n], twin).wait_recv()

    for k in range(1, NY):
        y_wait(0, k, xc.at[k])
    for k in range(NY):
        xt[:, k * tok:(k + 1) * tok] = xc[k].T
    other = zh * 2 + (1 - core)
    otherfar = (1 - zh) * 2 + (1 - core)
    c_wait(0, wfull.at[block(other), :])
    c_wait(1, sfull.at[block(other), :])
    c_wait(2, sfull.at[block(otherfar), :])

    igacc[...] = jnp.zeros_like(igacc)
    gcolv = gcol[:, 0:1]
    sgcolv = sgcol[:, 0:1]

    def stage_a(f):
        z_wait(f, wfull.at[block(far), cols[f]])
        go(remote(wfull.at[block(far), cols[f]], wfull.at[block(far), cols[f]],
                  csend.at[3 + f], crecv.at[3 + f], mate))
        c_wait(3 + f, wfull.at[block(otherfar), cols[f]])
        c = (gcolv * wfull[:, cols[f]].astype(F32) - sgcolv * sfull[:, cols[f]].astype(F32)).astype(BF16)
        for k in [1, 3, 2, 0]:
            part = jnp.dot(xc[k], c, preferred_element_type=F32)
            if k == 0:
                pself[f] = part
            else:
                back = NY - k
                psend[f, k] = part.astype(BF16)
                go(remote(psend.at[f, k], precv.at[f, back],
                          ysend.at[1 + f, back], yrecv.at[1 + f, back], at_y(back)))

    def stage_b(f):
        total = pself[f]
        for k in range(1, NY):
            y_wait(1 + f, k, precv.at[f, k])
            total = total + precv[f, k].astype(F32)
        rstd = rstd_ref[...]
        diff = total * (rstd * keep_ref[...])
        og[f, 0] = (diff * rstd).astype(BF16)
        for k in range(1, NY):
            go(remote(og.at[f, 0], og.at[f, k],
                      ysend.at[1 + CHUNKS + f, k], yrecv.at[1 + CHUNKS + f, k], at_y(k)))
        return jnp.sum(diff * diff, axis=1, keepdims=True)

    def stage_c(f):
        for k in range(1, NY):
            y_wait(1 + CHUNKS + f, k, og.at[f, k])
        ogf = og[f].reshape(NY * tok, width)
        g = jnp.dot(xt[...], ogf, preferred_element_type=F32)
        pself_gw = g
        gfull = gmsend.at[f]
        gfull[...] = pself_gw
        for n, b in enumerate([otherfar, other]):
            go(remote(gfull.at[block(b), :], gmrecv.at[f, n],
                      csend.at[3 + CHUNKS + 2 * f + n], crecv.at[3 + CHUNKS + 2 * f + n], mate))
        igacc[...] += lax.dot_general(ogf, wfull[:, cols[f]], (((1,), (1,)), ((), ())),
                                      preferred_element_type=F32)

    def stage_d(f):
        c_wait(3 + CHUNKS + 2 * f, gmrecv.at[f, 0])
        gzsend[f] = (gmsend[f, block(far), :] + gmrecv[f, 0]).astype(BF16)
        go(remote(gzsend.at[f], gzrecv.at[f], zsend.at[CHUNKS + f], zrecv.at[CHUNKS + f], twin))
        c_wait(3 + CHUNKS + 2 * f + 1, gmrecv.at[f, 1])
        gzkeep[f] = gmsend[f, block(mine), :] + gmrecv[f, 1]

    loss = jnp.zeros((tok, 1), F32)
    stage_a(0)
    for f in range(CHUNKS):
        loss = loss + stage_b(f)
        if f >= 1:
            stage_d(f - 1)
        if f + 1 < CHUNKS:
            stage_a(f + 1)
        stage_c(f)
    stage_d(CHUNKS - 1)
    loss_ref[...] = loss * (0.5 / feat)

    last = 1 + 2 * CHUNKS
    for k in range(NY):
        igsend[k] = igacc[k * tok:(k + 1) * tok, :].astype(BF16)
        if k:
            back = NY - k
            go(remote(igsend.at[k], igrecv.at[y],
                      ysend.at[last, back], yrecv.at[last, back], at_y(back)))
    igrecv[y] = igsend[0]
    for k in range(1, NY):
        y_wait(last, k, igrecv.at[lax.rem(y - k + NY, NY)])
    rstd = rstd_ref[...]
    mean = jnp.zeros((tok, 1), F32)
    for q in range(NY):
        scaled = igrecv[q].astype(F32) * grow[q]
        mean = mean + jnp.sum(scaled * x4[q].astype(F32), axis=1, keepdims=True)
    mean = mean * (rstd * (rstd / dim))
    for q in range(NY):
        scaled = igrecv[q].astype(F32) * grow[q]
        gt_ref[:, q * chans:(q + 1) * chans] = (scaled - x4[q].astype(F32) * mean).astype(BF16)

    scale = gcol[block(mine), 0:1] * (1.0 / (16.0 * tok) ** 0.5)
    for f in range(CHUNKS):
        z_wait(CHUNKS + f, gzrecv.at[f])
        gw_ref[:, cols[f]] = (gzkeep[f] + gzrecv[f].astype(F32)) * scale
    for copy in sent:
        copy.wait_send()


def swap_stale(stale, sgain, partner, ngroups, nshard):
    def branch(m):
        def run(s, g):
            same = [(i, i ^ m) for i in range(ngroups)]
            cross = [(i * nshard + d, (i ^ m) * nshard + (d ^ 2))
                     for i in range(ngroups) for d in range(nshard)]
            return (lax.ppermute(s, "group", same),
                    lax.ppermute(s, ("group", "fsdp"), cross),
                    lax.ppermute(g, "group", same))
        return run

    return lax.switch(partner[0] - 1, [branch(m) for m in range(1, ngroups)], stale, sgain)


def body(ngroups, nshard, tokens, token_ids, weight, stale_weight, gain, stale_gain, partner):
    x = tokens[0]
    w = weight[0]
    tok, dim = x.shape
    rows, feat = w.shape
    chans = dim // NY
    width = feat // CHUNKS
    y = lax.axis_index("fsdp") // 4
    sg = lax.dynamic_slice(stale_gain, (0, y * chans), (1, chans))
    sa, sb, sg = swap_stale(stale_weight[0], sg, partner, ngroups, nshard)
    keep = (token_ids[0] != 0).astype(F32)[:, None]
    vm = pl.BlockSpec(memory_space=pltpu.VMEM)
    gw, gt, loss = pl.pallas_call(
        step_kernel,
        out_shape=(
            jax.ShapeDtypeStruct((rows, feat), F32),
            jax.ShapeDtypeStruct((tok, dim), BF16),
            jax.ShapeDtypeStruct((tok, 1), F32),
        ),
        in_specs=[vm] * 7,
        out_specs=(vm, vm, vm),
        scratch_shapes=[
            pltpu.VMEM((NY, tok, chans), BF16),
            pltpu.VMEM((NY, tok, chans), BF16),
            pltpu.VMEM((chans, NY * tok), BF16),
            pltpu.VMEM((chans, feat), BF16),
            pltpu.VMEM((chans, feat), BF16),
            pltpu.VMEM((chans, 128), F32),
            pltpu.VMEM((chans, 128), F32),
            pltpu.VMEM((NY, 1, chans), F32),
            pltpu.VMEM((CHUNKS, tok, width), F32),
            pltpu.VMEM((CHUNKS, NY, tok, width), BF16),
            pltpu.VMEM((CHUNKS, NY, tok, width), BF16),
            pltpu.VMEM((CHUNKS, NY, tok, width), BF16),
            pltpu.VMEM((NY * tok, chans), F32),
            pltpu.VMEM((NY, tok, chans), BF16),
            pltpu.VMEM((NY, tok, chans), BF16),
            pltpu.VMEM((CHUNKS, chans, width), F32),
            pltpu.VMEM((CHUNKS, 2, rows, width), F32),
            pltpu.VMEM((CHUNKS, rows, width), F32),
            pltpu.VMEM((CHUNKS, rows, width), BF16),
            pltpu.VMEM((CHUNKS, rows, width), BF16),
            pltpu.VMEM((tok, 1), F32),
            pltpu.SemaphoreType.DMA((2 + 2 * CHUNKS, NY)),
            pltpu.SemaphoreType.DMA((2 + 2 * CHUNKS, NY)),
            pltpu.SemaphoreType.DMA((3 + 3 * CHUNKS,)),
            pltpu.SemaphoreType.DMA((3 + 3 * CHUNKS,)),
            pltpu.SemaphoreType.DMA((2 * CHUNKS,)),
            pltpu.SemaphoreType.DMA((2 * CHUNKS,)),
        ],
        compiler_params=pltpu.CompilerParams(
            collective_id=0, has_side_effects=True, vmem_limit_bytes=48 * 2**20
        ),
        name="codistill_step",
    )(x, keep, w, sa, sb, gain, sg)
    return gw[None], gt[None], loss[:, 0][None]


def solution(mesh):
    return jax.shard_map(
        functools.partial(body, mesh.shape["group"], mesh.shape["fsdp"]),
        mesh=mesh,
        in_specs=(
            P("group", "fsdp", None),
            P("group", "fsdp"),
            P("group", "fsdp", None),
            P("group", "fsdp", None),
            P("group", None),
            P("group", None),
            P(),
        ),
        out_specs=(P("group", "fsdp", None), P("group", "fsdp", None), P("group", "fsdp")),
        check_vma=False,
    )
```

time: 433 us -> 149 us (0.34)
  the two profiles are of different devices: /device:TPU:1 before, /device:TPU:33 now
where the time goes in v1:
time: 149 us
  Pallas kernels  101 us (68%)
  starting transfers between devices  23.8 us (16%)
  waiting for transfers between devices  18.6 us (12%)
  local copies, waits for them, and re-layouts  2.9 us (2%)
    pallas_call x1, Pallas kernels, body(): pl.pallas_call(step_kernel, out_shape=(jax.ShapeDtypeStruct((rows, feat),...  101 us
    ppermute x1, starting transfers between devices, run(): lax.ppermute(s, ('group', 'fsdp'), cross)  17 us
    ppermute x1, waiting for transfers between devices, run(): lax.ppermute(s, ('group', 'fsdp'), cross)  14.1 us
    ppermute x1, starting transfers between devices, run(): lax.ppermute(g, 'group', same)  4.65 us
    ppermute x1, waiting for transfers between devices, run(): lax.ppermute(g, 'group', same)  4.52 us
  transfers between devices with their start and end apart: 3, of which 2 were waited for; matrix products, arithmetic and copies ran while one was open for 0% of the time, Pallas kernels for 0%

profile of v1, /device:TPU:33, one launch (start us, length us, event | category | flops | bytes accessed | tf_op | source)
XLA Modules:
  0.0 148.9 jit_solution(3553817922410483793)
XLA Ops:
  0.6 0.0 copy-start
  0.6 0.0 copy-start.2
  1.4 0.7 fusion
  2.0 0.0 copy-done
  2.0 0.1 constant_dynamic-slice_fusion
  2.1 0.1 copy.11.keep_ref
  2.2 0.0 copy-start.3
  2.2 42.4 %conditional.1 = (bf16[144,1024]{1,0:T(8,128)(2,1)}, bf16[144,1024]{1,0:T(8,128)(2,1)}, bf16[1,576]{1,0:T(2,128)(2,1)}) conditional(s32[]{:T(128)} %bitcast.3, (bf16[144,1024]{1,0:T(8,128)(2,1)}, bf16[1,576]{1,0:T(2,128)(2,1)S(1)}) %tuple.182, (bf16[144,1024]{1,0:T(8,128)(2,1)}, ...), branch_computations={%region_0.1_spmd, %region_1.2_spmd, %region_2.3_spmd, %region_3.4_... | conditional | bytes 2364048 | solution.py:212
  2.3 17.0 %collective-permute-start.4 = (bf16[144,1024]{1,0:T(8,128)(2,1)}, bf16[144,1024]{1,0:T(8,128)(2,1)}, u32[]{:S(2)}, u32[]{:S(2)}) collective-permute-start(bf16[144,1024]{1,0:T(8,128)(2,1)} %get-tuple-element.126), channel_id=1, source_target_pairs={{0,34},{1,35},{2,32},{3,33},{4,38},{5,39},{6,36},{7,37},{8,42},{9,... | collective-permute-start | bytes 884744 | tf_op jit(solution)/shard_map/cond/branch_1_fun/ppermute | solution.py:208
  19.3 2.1 %collective-permute-start.3 = (bf16[144,1024]{1,0:T(8,128)(2,1)}, bf16[144,1024]{1,0:T(8,128)(2,1)}, u32[]{:S(2)}, u32[]{:S(2)}) collective-permute-start(bf16[144,1024]{1,0:T(8,128)(2,1)} %get-tuple-element.126), channel_id=1, source_target_pairs={{0,32},{16,48},{32,0},{48,16},{64,96},{80,112},{96,64},{112,80},{1... | collective-permute-start | bytes 884744 | tf_op jit(solution)/shard_map/cond/branch_1_fun/ppermute | solution.py:207
  21.4 4.7 %collective-permute-start.5 = (bf16[1,576]{1,0:T(2,128)(2,1)S(1)}, bf16[1,576]{1,0:T(2,128)(2,1)}, u32[]{:S(2)}, u32[]{:S(2)}) collective-permute-start(bf16[1,576]{1,0:T(2,128)(2,1)S(1)} %get-tuple-element.127), channel_id=1, source_target_pairs={{0,32},{16,48},{32,0},{48,16},{64,96},{80,112},{96,64},{112,80},{1... | collective-permute-start | bytes 3464 | tf_op jit(solution)/shard_map/cond/branch_1_fun/ppermute | solution.py:209
  26.1 4.5 %collective-permute-done.5 = bf16[1,576]{1,0:T(2,128)(2,1)} collective-permute-done((bf16[1,576]{1,0:T(2,128)(2,1)S(1)}, bf16[1,576]{1,0:T(2,128)(2,1)}, u32[]{:S(2)}, u32[]{:S(2)}) %collective-permute-start.5) | collective-permute-done | bytes 1184 | tf_op jit(solution)/shard_map/cond/branch_1_fun/ppermute | solution.py:209
  30.6 14.1 %collective-permute-done.4 = bf16[144,1024]{1,0:T(8,128)(2,1)} collective-permute-done((bf16[144,1024]{1,0:T(8,128)(2,1)}, bf16[144,1024]{1,0:T(8,128)(2,1)}, u32[]{:S(2)}, u32[]{:S(2)}) %collective-permute-start.4) | collective-permute-done | bytes 294944 | tf_op jit(solution)/shard_map/cond/branch_1_fun/ppermute | solution.py:208
  44.7 0.0 collective-permute-done.3
  44.7 0.0 copy-done.2
  44.7 0.0 copy-done.3
  44.7 0.0 copy-start.1
  44.7 1.1 copy-done.1
  45.7 100.9 %codistill_step.1 = (f32[144,1024]{1,0:T(8,128)S(1)}, bf16[128,2304]{1,0:T(8,128)(2,1)S(1)}, f32[128,1]{1,0:T(8,128)S(1)}) custom-call(bf16[128,2304]{1,0:T(8,128)(2,1)S(1)} %bitcast.10, f32[128,1]{1,0:T(8,128)S(1)} %copy.11.keep_ref, bf16[144,1024]{1,0:T(8,128)(2,1)S(1)} %bitcast.13, bf16[144,1024]{1,0:T(8,128)(2,1)} %get-tuple-element.195.sa_ref, ...), custom_call_target="tpu_custom_call" | custom-call | tf_op jit(solution)/shard_map/codistill_step/pallas_call | solution.py:227
  146.7 0.6 reduce
  147.3 0.8 copy.107
  148.1 0.8 copy.108
Async XLA Ops:
  0.6 1.4 copy-start
  0.6 44.0 %copy-start.2 = (bf16[1,144,1024]{2,1,0:T(8,128)(2,1)S(1)}, bf16[1,144,1024]{2,1,0:T(8,128)(2,1)}, u32[]{:S(2)}) copy-start(bf16[1,144,1024]{2,1,0:T(8,128)(2,1)} %param.40) | copy-start | bytes 884740
  2.2 42.4 %copy-start.3 = (bf16[1,2304]{1,0:T(2,128)(2,1)S(1)}, bf16[1,2304]{1,0:T(2,128)(2,1)}, u32[]{:S(2)}) copy-start(bf16[1,2304]{1,0:T(2,128)(2,1)} %gain_ref.1) | copy-start | bytes 13828
  2.3 42.4 %collective-permute-start.4 = (bf16[144,1024]{1,0:T(8,128)(2,1)}, bf16[144,1024]{1,0:T(8,128)(2,1)}, u32[]{:S(2)}, u32[]{:S(2)}) collective-permute-start(bf16[144,1024]{1,0:T(8,128)(2,1)} %get-tuple-element.126), channel_id=1, source_target_pairs={{0,34},{1,35},{2,32},{3,33},{4,38},{5,39},{6,36},{7,37},{8,42},{9,... | collective-permute-start | bytes 884744 | tf_op jit(solution)/shard_map/cond/branch_1_fun/ppermute | solution.py:208
  19.3 25.4 %collective-permute-start.3 = (bf16[144,1024]{1,0:T(8,128)(2,1)}, bf16[144,1024]{1,0:T(8,128)(2,1)}, u32[]{:S(2)}, u32[]{:S(2)}) collective-permute-start(bf16[144,1024]{1,0:T(8,128)(2,1)} %get-tuple-element.126), channel_id=1, source_target_pairs={{0,32},{16,48},{32,0},{48,16},{64,96},{80,112},{96,64},{112,80},{1... | collective-permute-start | bytes 884744 | tf_op jit(solution)/shard_map/cond/branch_1_fun/ppermute | solution.py:207
  21.4 9.2 %collective-permute-start.5 = (bf16[1,576]{1,0:T(2,128)(2,1)S(1)}, bf16[1,576]{1,0:T(2,128)(2,1)}, u32[]{:S(2)}, u32[]{:S(2)}) collective-permute-start(bf16[1,576]{1,0:T(2,128)(2,1)S(1)} %get-tuple-element.127), channel_id=1, source_target_pairs={{0,32},{16,48},{32,0},{48,16},{64,96},{80,112},{96,64},{112,80},{1... | collective-permute-start | bytes 3464 | tf_op jit(solution)/shard_map/cond/branch_1_fun/ppermute | solution.py:209
  44.7 1.1 copy-start.1

commit v2 on v0

v2 whole, which is shorter than its diff:
```python
import functools

import jax
import jax.numpy as jnp
from jax import lax
from jax.experimental import pallas as pl
from jax.experimental.pallas import tpu as pltpu
from jax.sharding import PartitionSpec as P

MESH = pl.DeviceIdType.MESH
NY = 4
CHUNKS = 4
EARLY = 2
F32 = jnp.float32
BF16 = jnp.bfloat16
VM = pl.BlockSpec(memory_space=pltpu.VMEM)


def flip_bits(index, m):
    bit = 1
    while bit <= m:
        if m & bit:
            index = index + bit * (1 - 2 * lax.rem(index // bit, 2))
        bit *= 2
    return index


class Place:
    def __init__(self, rows):
        self.rows = rows
        self.grp = lax.axis_index("group")
        self.me = lax.axis_index("fsdp")
        self.y = self.me // 4
        self.mine = lax.rem(self.me, 4)
        zh = self.mine // 2
        core = lax.rem(self.mine, 2)
        self.far = (1 - zh) * 2 + core
        self.other = zh * 2 + (1 - core)
        self.otherfar = (1 - zh) * 2 + (1 - core)
        self.mate = (self.grp, self.y * 4 + self.other)
        self.twin = (self.grp, self.y * 4 + self.far)

    def at_y(self, k):
        return (self.grp, lax.rem(self.y + k, NY) * 4 + self.mine)

    def block(self, b):
        return pl.ds(pl.multiple_of(b * self.rows, 16), self.rows)

    def greet(self, peers):
        barrier = pltpu.get_barrier_semaphore()
        for peer in peers:
            pl.semaphore_signal(barrier, inc=1, device_id=peer, device_id_type=MESH)
        return lambda: pl.semaphore_wait(barrier, len(peers))


def remote(src, dst, send, recv, dev):
    return pltpu.make_async_remote_copy(
        src_ref=src, dst_ref=dst, send_sem=send, recv_sem=recv,
        device_id=dev, device_id_type=MESH,
    )


def exchange_kernel(
    m,
    x_ref, w_ref, s_ref, sgain_ref,
    xc, wfull, sfull, sgrecv,
    x4, sgrow,
    ysend, yrecv, csend, crecv, zsend, zrecv,
):
    tok, dim = x_ref.shape
    rows, feat = w_ref.shape
    chans = dim // NY
    early = feat * EARLY // CHUNKS
    p = Place(rows)
    partner = flip_bits(p.grp, m)
    near = (partner, p.me)
    cross = (partner, p.y * 4 + p.far)
    peers = [near, cross, p.twin, p.mate] + [p.at_y(k) for k in range(1, NY)]
    arrive = p.greet(peers)
    sent = []

    def go(copy):
        copy.start()
        sent.append(copy)

    for q in range(NY):
        sgrow[q] = sgain_ref[:, q * chans:(q + 1) * chans].astype(F32)

    def cut(i, carry):
        at = pl.ds(pl.multiple_of(i * 16, 16), 16)
        for q in range(NY):
            x4[q, at, :] = x_ref[at, q * chans:(q + 1) * chans]
        return carry

    lax.fori_loop(0, tok // 16, cut, 0)
    arrive()

    mine = p.block(p.mine)
    go(remote(sgrow.at[p.y], sgrecv, zsend.at[3], zrecv.at[3], near))
    go(remote(s_ref, sfull.at[mine, :], zsend.at[0], zrecv.at[0], cross))
    go(remote(s_ref, sfull.at[mine, :], zsend.at[1], zrecv.at[1], near))
    if early:
        go(remote(w_ref.at[:, 0:early], wfull.at[mine, 0:early], zsend.at[2], zrecv.at[2], p.twin))
    go(remote(w_ref, wfull.at[mine, :], csend.at[0], crecv.at[0], p.mate))
    for k in range(1, NY):
        go(remote(x4.at[lax.rem(p.y + k, NY)], xc.at[k], ysend.at[k], yrecv.at[k], p.at_y(k)))
    local = [
        pltpu.make_async_copy(w_ref, wfull.at[mine, :], csend.at[4]),
        pltpu.make_async_copy(x4.at[p.y], xc.at[0], csend.at[5]),
    ]
    for copy in local:
        copy.start()

    far = p.block(p.far)
    arrivals = [(1, sfull.at[mine, :]), (0, sfull.at[far, :])]
    if early:
        arrivals.append((2, wfull.at[far, 0:early]))
    for n, ref in arrivals:
        remote(ref, ref, zsend.at[n], zrecv.at[n], p.twin).wait_recv()
        go(remote(ref, ref, csend.at[1 + n], crecv.at[1 + n], p.mate))

    remote(sgrecv, sgrecv, zsend.at[3], zrecv.at[3], near).wait_recv()
    for k in range(1, NY):
        remote(xc.at[k], xc.at[k], ysend.at[k], yrecv.at[k], p.at_y(k)).wait_recv()
    other = p.block(p.other)
    otherfar = p.block(p.otherfar)
    landed = [(0, wfull.at[other, :]), (2, sfull.at[other, :]), (1, sfull.at[otherfar, :])]
    if early:
        landed.append((3, wfull.at[otherfar, 0:early]))
    for n, ref in landed:
        remote(ref, ref, csend.at[n], crecv.at[n], p.mate).wait_recv()
    for copy in local:
        copy.wait()
    for copy in sent:
        copy.wait_send()


def exchange_for(m, x, w, s, sgain):
    tok, dim = x.shape
    rows, feat = w.shape
    chans = dim // NY
    return pl.pallas_call(
        functools.partial(exchange_kernel, m),
        out_shape=(
            jax.ShapeDtypeStruct((NY, tok, chans), BF16),
            jax.ShapeDtypeStruct((chans, feat), BF16),
            jax.ShapeDtypeStruct((chans, feat), BF16),
            jax.ShapeDtypeStruct((1, chans), F32),
        ),
        in_specs=[VM] * 4,
        out_specs=(VM,) * 4,
        scratch_shapes=[
            pltpu.VMEM((NY, tok, chans), BF16),
            pltpu.VMEM((NY, 1, chans), F32),
            pltpu.SemaphoreType.DMA((NY,)),
            pltpu.SemaphoreType.DMA((NY,)),
            pltpu.SemaphoreType.DMA((6,)),
            pltpu.SemaphoreType.DMA((6,)),
            pltpu.SemaphoreType.DMA((4,)),
            pltpu.SemaphoreType.DMA((4,)),
        ],
        compiler_params=pltpu.CompilerParams(
            collective_id=m, has_side_effects=True, vmem_limit_bytes=16 * 2**20
        ),
        name="exchange",
    )(x, w, s, sgain)


def step_kernel(
    x_ref, ids_ref, w_ref, gain_ref, xc, wfull, sfull, sg_ref,
    gw_ref, gt_ref, loss_ref,
    xt, wlate, cfull, gcol, sgcol, grow,
    pself, psend, precv, og, igacc, igsend, igrecv,
    gmsend, gmrecv, gzkeep, gzsend, gzrecv, rstd_ref, keep_ref,
    ysend, yrecv, csend, crecv, zsend, zrecv,
):
    tok, dim = x_ref.shape
    rows, feat = w_ref.shape
    chans = dim // NY
    width = feat // CHUNKS
    p = Place(rows)
    y = p.y
    arrive = p.greet([p.twin, p.mate] + [p.at_y(k) for k in range(1, NY)])
    sent = []

    def go(copy):
        copy.start()
        sent.append(copy)

    def y_wait(n, k, ref):
        remote(ref, ref, ysend.at[n, k], yrecv.at[n, k], p.at_y(k)).wait_recv()

    def c_wait(n, ref):
        remote(ref, ref, csend.at[n], crecv.at[n], p.mate).wait_recv()

    def z_wait(n, ref):
        remote(ref, ref, zsend.at[n], zrecv.at[n], p.twin).wait_recv()

    block = p.block
    cols = [pl.ds(f * width, width) for f in range(CHUNKS)]

    for q in range(NY):
        grow[q] = gain_ref[:, q * chans:(q + 1) * chans].astype(F32)
    gcol[...] = jnp.broadcast_to(grow[y], (128, chans)).T
    sgcol[...] = jnp.broadcast_to(sg_ref[...], (128, chans)).T

    def weights(f):
        return wfull[:, cols[f]] if f < EARLY else wlate[f - EARLY]

    def stage_a(f):
        if f >= EARLY:
            n = f - EARLY
            z_wait(n, wlate.at[n, block(p.far), :])
            go(remote(wlate.at[n, block(p.far), :], wlate.at[n, block(p.far), :],
                      csend.at[n], crecv.at[n], p.mate))
            for b in (p.mine, p.other):
                wlate[n, block(b), :] = wfull[block(b), cols[f]]
            c_wait(n, wlate.at[n, block(p.otherfar), :])
        c = (gcol[:, 0:1] * weights(f).astype(F32) - sgcol[:, 0:1] * sfull[:, cols[f]].astype(F32))
        cfull[...] = c.astype(BF16)
        for k in [2, 1, 3, 0]:
            part = jnp.dot(xc[k], cfull[...], preferred_element_type=F32)
            if k == 0:
                pself[f] = part
            else:
                back = NY - k
                psend[f, k] = part.astype(BF16)
                if f == 0 and k == 2:
                    arrive()
                    for n in range(CHUNKS - EARLY):
                        go(remote(w_ref.at[:, cols[EARLY + n]], wlate.at[n, block(p.mine), :],
                                  zsend.at[n], zrecv.at[n], p.twin))
                go(remote(psend.at[f, k], precv.at[f, back],
                          ysend.at[f, back], yrecv.at[f, back], p.at_y(back)))

    def stage_b(f):
        total = pself[f]
        for k in range(1, NY):
            y_wait(f, k, precv.at[f, k])
            total = total + precv[f, k].astype(F32)
        rstd = rstd_ref[...]
        diff = total * (rstd * keep_ref[...])
        og[f, 0] = (diff * rstd).astype(BF16)
        for k in [2, 1, 3]:
            go(remote(og.at[f, 0], og.at[f, k],
                      ysend.at[CHUNKS + f, k], yrecv.at[CHUNKS + f, k], p.at_y(k)))
        return jnp.sum(diff * diff, axis=1, keepdims=True)

    def stage_c(f):
        first = CHUNKS + 2 * f
        for k in range(1, NY):
            y_wait(CHUNKS + f, k, og.at[f, k])
        ogf = og[f].reshape(NY * tok, width)
        gmsend[f] = jnp.dot(xt[...], ogf, preferred_element_type=F32)
        for n, b in enumerate([p.otherfar, p.other]):
            go(remote(gmsend.at[f, block(b), :], gmrecv.at[f, n],
                      csend.at[first + n], crecv.at[first + n], p.mate))
        igacc[...] += lax.dot_general(ogf, weights(f), (((1,), (1,)), ((), ())),
                                      preferred_element_type=F32)
        c_wait(first, gmrecv.at[f, 0])
        gzsend[f] = (gmsend[f, block(p.far), :] + gmrecv[f, 0]).astype(BF16)
        go(remote(gzsend.at[f], gzrecv.at[f], zsend.at[CHUNKS + f], zrecv.at[CHUNKS + f], p.twin))
        c_wait(first + 1, gmrecv.at[f, 1])
        gzkeep[f] = gmsend[f, block(p.mine), :] + gmrecv[f, 1]

    stage_a(0)
    xf = x_ref[...].astype(F32)
    rstd_ref[...] = lax.rsqrt(jnp.mean(xf * xf, axis=1, keepdims=True) + 1e-06)
    keep = (ids_ref[...] != 0).astype(F32)
    keep_ref[...] = jnp.broadcast_to(keep, (tok, tok)).T[:, 0:1]
    igacc[...] = jnp.zeros_like(igacc)
    for k in range(NY):
        xt[:, k * tok:(k + 1) * tok] = xc[k].T
    loss = jnp.zeros((tok, 1), F32)
    for f in range(CHUNKS):
        if f + 1 < CHUNKS and f + 1 < EARLY:
            stage_a(f + 1)
        loss = loss + stage_b(f)
        if f + 1 < CHUNKS and f + 1 >= EARLY:
            if f >= 1:
                stage_c(f - 1)
            stage_a(f + 1)
        elif f >= 1:
            stage_c(f - 1)
    stage_c(CHUNKS - 1)
    loss_ref[...] = jnp.broadcast_to(loss * (0.5 / feat), (tok, tok)).T[0:1, :]

    last = 2 * CHUNKS
    for k in [2, 1, 3, 0]:
        igsend[k] = igacc[k * tok:(k + 1) * tok, :].astype(BF16)
        if k:
            back = NY - k
            go(remote(igsend.at[k], igrecv.at[y],
                      ysend.at[last, back], yrecv.at[last, back], p.at_y(back)))
    igrecv[y] = igsend[0]
    for k in range(1, NY):
        y_wait(last, k, igrecv.at[lax.rem(y - k + NY, NY)])
    rstd = rstd_ref[...]
    mean = jnp.zeros((tok, 1), F32)
    for q in range(NY):
        scaled = igrecv[q].astype(F32) * grow[q]
        xq = x_ref[:, q * chans:(q + 1) * chans].astype(F32)
        mean = mean + jnp.sum(scaled * xq, axis=1, keepdims=True)
    mean = mean * (rstd * (rstd / dim))
    for q in range(NY):
        scaled = igrecv[q].astype(F32) * grow[q]
        xq = x_ref[:, q * chans:(q + 1) * chans].astype(F32)
        gt_ref[:, q * chans:(q + 1) * chans] = (scaled - xq * mean).astype(BF16)

    scale = gcol[block(p.mine), 0:1] * (1.0 / (16.0 * tok) ** 0.5)
    for f in range(CHUNKS):
        z_wait(CHUNKS + f, gzrecv.at[f])
        gw_ref[:, cols[f]] = (gzkeep[f] + gzrecv[f].astype(F32)) * scale
    for copy in sent:
        copy.wait_send()


def step(x, ids, w, gain, xc, wfull, sfull, sg):
    tok, dim = x.shape
    rows, feat = w.shape
    chans = dim // NY
    width = feat // CHUNKS
    return pl.pallas_call(
        step_kernel,
        out_shape=(
            jax.ShapeDtypeStruct((rows, feat), F32),
            jax.ShapeDtypeStruct((tok, dim), BF16),
            jax.ShapeDtypeStruct((1, tok), F32),
        ),
        in_specs=[VM] * 8,
        out_specs=(VM,) * 3,
        scratch_shapes=[
            pltpu.VMEM((chans, NY * tok), BF16),
            pltpu.VMEM((max(CHUNKS - EARLY, 1), chans, width), BF16),
            pltpu.VMEM((chans, width), BF16),
            pltpu.VMEM((chans, 128), F32),
            pltpu.VMEM((chans, 128), F32),
            pltpu.VMEM((NY, 1, chans), F32),
            pltpu.VMEM((CHUNKS, tok, width), F32),
            pltpu.VMEM((CHUNKS, NY, tok, width), BF16),
            pltpu.VMEM((CHUNKS, NY, tok, width), BF16),
            pltpu.VMEM((CHUNKS, NY, tok, width), BF16),
            pltpu.VMEM((NY * tok, chans), F32),
            pltpu.VMEM((NY, tok, chans), BF16),
            pltpu.VMEM((NY, tok, chans), BF16),
            pltpu.VMEM((CHUNKS, chans, width), F32),
            pltpu.VMEM((CHUNKS, 2, rows, width), F32),
            pltpu.VMEM((CHUNKS, rows, width), F32),
            pltpu.VMEM((CHUNKS, rows, width), BF16),
            pltpu.VMEM((CHUNKS, rows, width), BF16),
            pltpu.VMEM((tok, 1), F32),
            pltpu.VMEM((tok, 1), F32),
            pltpu.SemaphoreType.DMA((1 + 2 * CHUNKS, NY)),
            pltpu.SemaphoreType.DMA((1 + 2 * CHUNKS, NY)),
            pltpu.SemaphoreType.DMA((3 * CHUNKS,)),
            pltpu.SemaphoreType.DMA((3 * CHUNKS,)),
            pltpu.SemaphoreType.DMA((2 * CHUNKS,)),
            pltpu.SemaphoreType.DMA((2 * CHUNKS,)),
        ],
        compiler_params=pltpu.CompilerParams(
            collective_id=0, has_side_effects=True, vmem_limit_bytes=40 * 2**20
        ),
        name="codistill_step",
    )(x, ids, w, gain, xc, wfull, sfull, sg)


def body(ngroups, tokens, token_ids, weight, stale_weight, gain, stale_gain, partner):
    branches = [functools.partial(exchange_for, m) for m in range(1, ngroups)]
    x, w = tokens[0], weight[0]
    xc, wfull, sfull, sg = lax.switch(
        partner[0] - 1, branches, x, w, stale_weight[0], stale_gain
    )
    gw, gt, loss = step(x, token_ids, w, gain, xc, wfull, sfull, sg)
    return gw[None], gt[None], loss


def solution(mesh):
    return jax.shard_map(
        functools.partial(body, mesh.shape["group"]),
        mesh=mesh,
        in_specs=(
            P("group", "fsdp", None),
            P("group", "fsdp"),
            P("group", "fsdp", None),
            P("group", "fsdp", None),
            P("group", None),
            P("group", None),
            P(),
        ),
        out_specs=(P("group", "fsdp", None), P("group", "fsdp", None), P("group", "fsdp")),
        check_vma=False,
    )
```

time: 433 us -> 122 us (0.28)
  waiting for transfers between devices: 345 us -> 0 us
  Pallas kernels: 0 us -> 117 us
  starting transfers between devices: 52.8 us -> 0 us
  matrix products: 15 us -> 0 us
  between operations: 14.8 us -> 1.33 us
  other arithmetic: 5.03 us -> 0 us
    all_gather x3 -> x0, waiting for transfers between devices: 201 us -> none  [the longest x1 103 us: body(): lax.all_gather(teacher_w, 'fsdp', axis=0, tiled=True)]
    ppermute x10 -> x0, waiting for transfers between devices: 123 us -> none  [partner_2(): lax.ppermute(array, axis, [(i, i ^ 1 << apart) for i in range(lax.axis_si...]
    pallas_call x0 -> x2, Pallas kernels: none -> 117 us  [the longest x1 63 us: exchange_for(): pl.pallas_call(functools.partial(exchange_kernel, m), out_shape=(jax.Shap...]
    ppermute x10 -> x0, starting transfers between devices: 48.7 us -> none  [partner_2(): lax.ppermute(array, axis, [(i, i ^ 1 << apart) for i in range(lax.axis_si...]
    all_to_all x1 -> x0, waiting for transfers between devices: 20.7 us -> none  [body(): lax.all_to_all(student_in, 'fsdp', split_axis=1, concat_axis=0, tiled=True)]
    dot_general x4 -> x0, matrix products: 15 us -> none  [the longest x1 4.12 us: body(): lax.dot_general(out_grad, full_rows, (((1,), (1,)), ((), ())), preferred_...]
  transfers between devices with their start and end apart: 14 -> 0, of which waited for: 13 -> 0; matrix products, arithmetic and copies ran while one was open for 3% -> 0% of each run, Pallas kernels for 0% -> 0%
where the time goes in v2:
time: 122 us; the launch traced here: 121 us
  Pallas kernels  117 us (96%)
  local copies, waits for them, and re-layouts  2.15 us (2%)
  between operations  1.33 us (1%)
    pallas_call x1, Pallas kernels, exchange_for(): pl.pallas_call(functools.partial(exchange_kernel, m), out_shape=(jax.Shap...  63 us
    pallas_call x1, Pallas kernels, step(): pl.pallas_call(step_kernel, out_shape=(jax.ShapeDtypeStruct((rows, feat),...  54 us

profile of v2, /device:TPU:1, one launch (start us, length us, event | category | flops | bytes accessed | tf_op | source)
XLA Modules:
  0.0 120.7 jit_solution(17843112831010658836)
XLA Ops:
  1.3 0.0 copy-start
  1.3 0.0 copy-start.1
  1.3 63.3 %conditional.1 = ((bf16[4,128,576]{2,1,0:T(8,128)(2,1)S(1)}, bf16[576,1024]{1,0:T(8,128)(2,1)S(1)}, bf16[576,1024]{1,0:T(8,128)(2,1)S(1)}, f32[1,576]{1,0:T(1,128)S(1)})) conditional(s32[]{:T(128)} %bitcast.2, (bf16[128,2304]{1,0:T(8,128)(2,1)}, bf16[144,1024]{1,0:T(8,128)(2,1)}, bf16[144,1024]{1,0:T(8,128)(2,1)}, ...), branch_computations={%region_0.0_spmd, %region_1.0_spmd, %region_2.0_spmd, %region_3.0_... | conditional | bytes 8 | solution.py:370
  1.4 63.0 %exchange.60 = (bf16[4,128,576]{2,1,0:T(8,128)(2,1)S(1)}, bf16[576,1024]{1,0:T(8,128)(2,1)S(1)}, bf16[576,1024]{1,0:T(8,128)(2,1)S(1)}, f32[1,576]{1,0:T(1,128)S(1)}) custom-call(bf16[128,2304]{1,0:T(8,128)(2,1)} %get-tuple-element.364.x_ref, bf16[144,1024]{1,0:T(8,128)(2,1)} %get-tuple-element.365.w_ref, bf16[144,1024]{1,0:T(8,128)(2,1)} %get-tuple-element.366.s_ref, ...), custom_call_target="tpu_custom_call" | custom-call | tf_op jit(solution)/shard_map/cond/branch_29_fun/exchange/pallas_call | solution.py:142
  64.6 0.0 copy-done
  64.6 0.0 copy-done.1
  64.6 54.0 %codistill_step.1 = (f32[144,1024]{1,0:T(8,128)S(1)}, bf16[128,2304]{1,0:T(8,128)(2,1)S(1)}, f32[1,128]{1,0:T(1,128)S(1)}) custom-call(bf16[128,2304]{1,0:T(8,128)(2,1)} %bitcast.40, s32[1,128]{1,0:T(1,128)S(1)} %copy-done.1, bf16[144,1024]{1,0:T(8,128)(2,1)} %bitcast.72, bf16[1,2304]{1,0:T(2,128)(2,1)S(1)} %copy-done, ...), custom_call_target="tpu_custom_call" | custom-call | tf_op jit(solution)/shard_map/codistill_step/pallas_call | solution.py:323
  118.6 0.8 copy.137
  119.4 0.8 copy.138
  120.2 0.5 copy.139
Async XLA Ops:
  1.3 63.3 %copy-start = (bf16[1,2304]{1,0:T(2,128)(2,1)S(1)}, bf16[1,2304]{1,0:T(2,128)(2,1)}, u32[]{:S(2)}) copy-start(bf16[1,2304]{1,0:T(2,128)(2,1)} %gain_ref.1) | copy-start | bytes 13828
  1.3 63.3 %copy-start.1 = (s32[1,128]{1,0:T(1,128)S(1)}, s32[1,128]{1,0:T(1,128)}, u32[]{:S(2)}) copy-start(s32[1,128]{1,0:T(1,128)} %ids_ref.1) | copy-start | bytes 1540

commit v3 on v0

v3 whole, which is shorter than its diff:
```python
import functools

import jax
import jax.numpy as jnp
from jax import lax
from jax.experimental import pallas as pl
from jax.experimental.pallas import tpu as pltpu
from jax.sharding import PartitionSpec as P

MESH = pl.DeviceIdType.MESH
NX = 4
NY = 4
CHUNKS = 4
UNROLL = True
AHEAD = 1
F32 = jnp.float32
BF16 = jnp.bfloat16
VM = pl.BlockSpec(memory_space=pltpu.VMEM)
SM = pl.BlockSpec(memory_space=pltpu.SMEM)


def flip_bits(index, m):
    bit = 1
    while bit <= m:
        if m & bit:
            index = index + bit * (1 - 2 * lax.rem(index // bit, 2))
        bit *= 2
    return index


def remote(src, dst, send, recv, dev):
    return pltpu.make_async_remote_copy(
        src_ref=src, dst_ref=dst, send_sem=send, recv_sem=recv,
        device_id=dev, device_id_type=MESH,
    )


def each(n, f, unroll=False):
    def go(i, carry):
        f(i)
        return carry

    lax.fori_loop(0, n, go, 0, unroll=unroll)


def rows16(i, base=0):
    return pl.ds(pl.multiple_of(base + i * 16, 16), 16)


def step_kernel(
    mz,
    partner_ref, x_ref, ids_ref, w_ref, s_ref, gain_ref, sgain_ref,
    gw_ref, gt_ref, loss_ref,
    x4, xc, xt, wfull, sfull, cfull, sx1, st1, sx2, st2,
    grow, sgrow, sgx, gcols,
    part, psend, precv, og, igacc, igsend, igrecv,
    gm, gmrecv, gzsend, gzrecv, rstd_ref, keep_ref, loss_acc,
    ysend, yrecv, csend, crecv, zsend, zrecv, xsend, xrecv,
):
    tok, dim = x_ref.shape
    rows, feat = w_ref.shape
    chans = dim // NY
    width = feat // CHUNKS
    grp = lax.axis_index("group")
    me = lax.axis_index("fsdp")
    y = me // 4
    mine = lax.rem(me, 4)
    zh = mine // 2
    core = lax.rem(mine, 2)
    far = (1 - zh) * 2 + core
    other = zh * 2 + (1 - core)
    otherfar = (1 - zh) * 2 + (1 - core)
    zpart = flip_bits(grp, mz * NX)
    mate = (grp, y * 4 + other)
    twin = (grp, y * 4 + far)
    near = (zpart, me)
    cross = (zpart, y * 4 + far)
    x1 = (flip_bits(grp, 1), me)
    x2 = (flip_bits(grp, 2), me)

    def at_y(k):
        return (grp, lax.rem(y + k, NY) * 4 + mine)

    def block(b):
        return pl.ds(pl.multiple_of(b * rows, 16), rows)

    def lanes(f):
        return pl.ds(pl.multiple_of(f * width, 128), width)

    IG, X = 2 * CHUNKS, 2 * CHUNKS + 1

    def y_copy(n, k, src, dst):
        return remote(src, dst, ysend.at[n, k], yrecv.at[n, k], at_y(k))

    def c_copy(n, f, src, dst):
        return remote(src, dst, csend.at[n, f], crecv.at[n, f], mate)

    def z_copy(n, f, src, dst, dev):
        return remote(src, dst, zsend.at[n, f], zrecv.at[n, f], dev)

    def x_copy(n, f, src, dst, dev):
        return remote(src, dst, xsend.at[n, f], xrecv.at[n, f], dev)

    def to_twin(f):
        z_copy(0, f, w_ref.at[:, lanes(f)], wfull.at[f, block(mine), :], twin).start()

    peers = [twin, mate, x1, x2] + [at_y(k) for k in range(1, NY)]
    if mz:
        peers += [near, cross]
    barrier = pltpu.get_barrier_semaphore()
    for peer in peers:
        pl.semaphore_signal(barrier, inc=1, device_id=peer, device_id_type=MESH)

    for q in range(NY):
        grow[q] = gain_ref[:, q * chans:(q + 1) * chans].astype(F32)
        sgrow[q] = sgain_ref[:, q * chans:(q + 1) * chans].astype(F32)

    def cut(i):
        at = rows16(i)
        xr = x_ref[at, :]
        for q in range(NY):
            x4[q, at, :] = xr[:, q * chans:(q + 1) * chans]
        xf = xr.astype(F32)
        rstd_ref[at, :] = lax.rsqrt(jnp.mean(xf * xf, axis=1, keepdims=True) + 1e-06)

    each(tok // 16, cut)
    pl.semaphore_wait(barrier, len(peers))

    x_copy(0, 0, sgrow.at[y], sgx.at[0], x1).start()

    def own(f):
        pl.when(f < AHEAD)(lambda: to_twin(f))
        x_copy(1, f, s_ref.at[:, lanes(f)], sx1.at[f], x1).start()
        c_copy(0, f, w_ref.at[:, lanes(f)], wfull.at[f, block(mine), :]).start()
        wfull[f, block(mine), :] = w_ref[:, lanes(f)]

    each(CHUNKS, own)

    def spread(k):
        y_copy(X, k, x4.at[lax.rem(y + k, NY)], xc.at[k]).start()

    each_k = lambda f: each(NY - 1, lambda i: f(i + 1))
    each_k(spread)
    xc[0] = x4[y]

    m = partner_ref[0]
    bit0 = lax.rem(m, 2) == 1
    bit1 = lax.rem(m // 2, 2) == 1
    x_copy(0, 0, sgrow.at[y], sgx.at[0], x1).wait_recv()
    sgx[1] = jnp.where(bit0, sgx[0], sgrow[y])
    x_copy(0, 1, sgx.at[1], sgx.at[2], x2).start()

    def first(f):
        x_copy(1, f, st1.at[f], sx1.at[f], x1).wait_recv()

        st1[f] = jnp.where(bit0, sx1[f], s_ref[:, lanes(f)])
        x_copy(2, f, st1.at[f], sx2.at[f], x2).start()

    each(CHUNKS, first)
    x_copy(0, 1, sgx.at[1], sgx.at[2], x2).wait_recv()
    sgx[3] = jnp.where(bit1, sgx[2], sgx[1])
    if mz:
        x_copy(0, 2, sgx.at[3], sgx.at[4], near).start()
    else:
        sgx[4] = sgx[3]

    def second(f):
        x_copy(2, f, st1.at[f], sx2.at[f], x2).wait_recv()

        st2[f] = jnp.where(bit1, sx2[f], st1[f])
        z_copy(2, f, st2.at[f], sfull.at[f, block(mine), :], cross).start()
        if mz:
            z_copy(1, f, st2.at[f], sfull.at[f, block(mine), :], near).start()
        else:
            sfull[f, block(mine), :] = st2[f]
        pl.when(f < CHUNKS - AHEAD)(lambda: to_twin(f + AHEAD))

    each(CHUNKS, second)

    keep = (ids_ref[...] != 0).astype(F32)
    keep_ref[...] = jnp.broadcast_to(keep, (tok, tok)).T[:, 0:1]
    loss_acc[...] = jnp.zeros_like(loss_acc)

    def clear(i):
        igacc[pl.ds(pl.multiple_of(i * tok, 128), tok), :] = jnp.zeros((tok, chans), F32)

    each(NY, clear)
    each_k(lambda k: y_copy(X, k, xc.at[k], xc.at[k]).wait_recv())

    def turn(k):
        xt[:, pl.ds(pl.multiple_of(k * tok, 128), tok)] = xc[k].T

    each(NY, turn)

    if mz:
        x_copy(0, 2, sgx.at[3], sgx.at[4], near).wait()
    sgx[3] = grow[y]

    def column(j):
        gcols[j] = jnp.broadcast_to(sgx[3 + j], (128, chans)).T

    each(2, column, UNROLL)

    def stage_a(f):
        z_copy(0, f, wfull.at[f, block(far), :], wfull.at[f, block(far), :], twin).wait_recv()
        c_copy(1, f, wfull.at[f, block(far), :], wfull.at[f, block(far), :]).start()
        if mz:
            z_copy(1, f, sfull.at[f, block(mine), :], sfull.at[f, block(mine), :], twin).wait_recv()
        z_copy(2, f, sfull.at[f, block(far), :], sfull.at[f, block(far), :], twin).wait_recv()

        def combine(n):
            b = mine + n * (far - mine)
            at = block(b)
            cfull[f, at, :] = (
                gcols[0, at, 0:1] * wfull[f, at, :].astype(F32)
                - gcols[1, at, 0:1] * sfull[f, at, :].astype(F32)
            ).astype(BF16)
            c_copy(2 + n, f, cfull.at[f, block(b), :], cfull.at[f, block(b), :]).start()

        each(2, combine)
        c_copy(0, f, wfull.at[f, block(other), :], wfull.at[f, block(other), :]).wait_recv()
        c_copy(1, f, wfull.at[f, block(otherfar), :], wfull.at[f, block(otherfar), :]).wait_recv()
        c_copy(2, f, cfull.at[f, block(other), :], cfull.at[f, block(other), :]).wait_recv()
        c_copy(3, f, cfull.at[f, block(otherfar), :], cfull.at[f, block(otherfar), :]).wait_recv()

        def product(i):
            k = lax.rem(i + 1, NY)
            got = jnp.dot(xc[k], cfull[f], preferred_element_type=F32)
            part[f, k] = got
            psend[f, k] = got.astype(BF16)

            @pl.when(i < NY - 1)
            def _():
                y_copy(f, NY - k, psend.at[f, k], precv.at[f, NY - k]).start()

        each(NY, product, UNROLL)

    def stage_b(f):
        each_k(lambda k: y_copy(f, k, precv.at[f, k], precv.at[f, k]).wait_recv())

        total = part[f, 0]
        for k in range(1, NY):
            total = total + precv[f, k].astype(F32)
        rstd = rstd_ref[...]
        diff = total * (rstd * keep_ref[...])
        og[f, 0] = (diff * rstd).astype(BF16)
        loss_acc[...] += jnp.sum(diff * diff, axis=1, keepdims=True)
        each_k(lambda k: y_copy(CHUNKS + f, k, og.at[f, 0], og.at[f, k]).start())

    def stage_c(f):
        each_k(lambda k: y_copy(CHUNKS + f, k, og.at[f, k], og.at[f, k]).wait_recv())

        def outer(j):
            b = ((1 - zh) + lax.rem(j, 2) * (2 * zh - 1)) * 2 + (1 - core) + (j // 2) * (2 * core - 1)
            gm[f, block(b), :] = jnp.dot(
                xt[block(b), :], og[f].reshape(NY * tok, width), preferred_element_type=F32
            )

            @pl.when(j < 2)
            def _():
                c_copy(4 + j, f, gm.at[f, block(b), :], gmrecv.at[f, j]).start()

        each(NY, outer, UNROLL)

        def back(k):
            at = pl.ds(pl.multiple_of(k * tok, 128), tok)
            igacc[at, :] += lax.dot_general(
                og[f, k], wfull[f], (((1,), (1,)), ((), ())), preferred_element_type=F32
            )

        each(NY, back, UNROLL)
        c_copy(4, f, gmrecv.at[f, 0], gmrecv.at[f, 0]).wait_recv()

        gzsend[f] = (gm[f, block(far), :] + gmrecv[f, 0]).astype(BF16)
        z_copy(3, f, gzsend.at[f], gzrecv.at[f], twin).start()
        c_copy(5, f, gmrecv.at[f, 1], gmrecv.at[f, 1]).wait_recv()

    def turnover(t):
        pl.when(t < CHUNKS)(lambda: stage_a(t))
        pl.when((t >= 1) & (t <= CHUNKS))(lambda: stage_b(t - 1))
        pl.when(t >= 2)(lambda: stage_c(t - 2))

    each(CHUNKS + 2, turnover)
    loss_ref[...] = jnp.broadcast_to(loss_acc[...] * (0.5 / feat), (tok, tok)).T[0:1, :]

    def home(i):
        k = lax.rem(i + 1, NY)
        at = pl.ds(pl.multiple_of(k * tok, 128), tok)
        igsend[k] = igacc[at, :].astype(BF16)

        @pl.when(i < NY - 1)
        def _():
            y_copy(IG, NY - k, igsend.at[k], igrecv.at[y]).start()

    each(NY, home)
    igrecv[y] = igsend[0]
    each_k(lambda k: y_copy(IG, k, igrecv.at[lax.rem(y - k + NY, NY)], igrecv.at[lax.rem(y - k + NY, NY)]).wait_recv())

    def tokens_back(i):
        at = rows16(i)
        rstd = rstd_ref[at, :]
        scaled = [igrecv[q, at, :].astype(F32) * grow[q] for q in range(NY)]
        xq = [x4[q, at, :].astype(F32) for q in range(NY)]
        mean = sum(jnp.sum(s * v, axis=1, keepdims=True) for s, v in zip(scaled, xq))
        mean = mean * (rstd * (rstd / dim))
        for q in range(NY):
            gt_ref[at, q * chans:(q + 1) * chans] = (scaled[q] - xq[q] * mean).astype(BF16)

    each(tok // 16, tokens_back)

    def finish(f):
        z_copy(3, f, gzrecv.at[f], gzrecv.at[f], twin).wait_recv()

        scale = gcols[0, block(mine), 0:1] * (1.0 / (16.0 * tok) ** 0.5)
        total = gm[f, block(mine), :] + gmrecv[f, 1] + gzrecv[f].astype(F32)
        gw_ref[:, lanes(f)] = total * scale

    each(CHUNKS, finish)

    x_copy(0, 0, sgrow.at[y], sgx.at[0], x1).wait_send()
    x_copy(0, 1, sgx.at[1], sgx.at[2], x2).wait_send()

    def left(f):
        for n in [0, 1, 2, 3] if mz else [0, 2, 3]:
            z_copy(n, f, gzsend.at[f], gzsend.at[f], twin).wait_send()
        for n in (1, 2):
            x_copy(n, f, st1.at[f], sx1.at[f], x1).wait_send()
        for n in range(4):
            c_copy(n, f, gzsend.at[f], gzsend.at[f]).wait_send()
        for n in range(2):
            c_copy(4 + n, f, gmrecv.at[f, n], gmrecv.at[f, n]).wait_send()

    each(CHUNKS, left)

    def left_y(k):
        each(2 * CHUNKS, lambda n: y_copy(n, k, og.at[0, 0], og.at[0, 0]).wait_send())
        for n in (IG, X):
            y_copy(n, k, igsend.at[0], igsend.at[0]).wait_send()

    each_k(left_y)


def step_for(mz, x, ids, w, s, gain, sgain, partner):
    tok, dim = x.shape
    rows, feat = w.shape
    chans = dim // NY
    width = feat // CHUNKS
    return pl.pallas_call(
        functools.partial(step_kernel, mz),
        out_shape=(
            jax.ShapeDtypeStruct((rows, feat), F32),
            jax.ShapeDtypeStruct((tok, dim), BF16),
            jax.ShapeDtypeStruct((1, tok), F32),
        ),
        in_specs=[SM] + [VM] * 6,
        out_specs=(VM,) * 3,
        scratch_shapes=[
            pltpu.VMEM((NY, tok, chans), BF16),
            pltpu.VMEM((NY, tok, chans), BF16),
            pltpu.VMEM((chans, NY * tok), BF16),
            pltpu.VMEM((CHUNKS, chans, width), BF16),
            pltpu.VMEM((CHUNKS, chans, width), BF16),
            pltpu.VMEM((CHUNKS, chans, width), BF16),
            pltpu.VMEM((CHUNKS, rows, width), BF16),
            pltpu.VMEM((CHUNKS, rows, width), BF16),
            pltpu.VMEM((CHUNKS, rows, width), BF16),
            pltpu.VMEM((CHUNKS, rows, width), BF16),
            pltpu.VMEM((NY, 1, chans), F32),
            pltpu.VMEM((NY, 1, chans), F32),
            pltpu.VMEM((5, 1, chans), F32),
            pltpu.VMEM((2, chans, 128), F32),
            pltpu.VMEM((CHUNKS, NY, tok, width), F32),
            pltpu.VMEM((CHUNKS, NY, tok, width), BF16),
            pltpu.VMEM((CHUNKS, NY, tok, width), BF16),
            pltpu.VMEM((CHUNKS, NY, tok, width), BF16),
            pltpu.VMEM((NY * tok, chans), F32),
            pltpu.VMEM((NY, tok, chans), BF16),
            pltpu.VMEM((NY, tok, chans), BF16),
            pltpu.VMEM((CHUNKS, chans, width), F32),
            pltpu.VMEM((CHUNKS, 2, rows, width), F32),
            pltpu.VMEM((CHUNKS, rows, width), BF16),
            pltpu.VMEM((CHUNKS, rows, width), BF16),
            pltpu.VMEM((tok, 1), F32),
            pltpu.VMEM((tok, 1), F32),
            pltpu.VMEM((tok, 1), F32),
            pltpu.SemaphoreType.DMA((2 + 2 * CHUNKS, NY)),
            pltpu.SemaphoreType.DMA((2 + 2 * CHUNKS, NY)),
            pltpu.SemaphoreType.DMA((6, CHUNKS)),
            pltpu.SemaphoreType.DMA((6, CHUNKS)),
            pltpu.SemaphoreType.DMA((4, CHUNKS)),
            pltpu.SemaphoreType.DMA((4, CHUNKS)),
            pltpu.SemaphoreType.DMA((3, max(CHUNKS, 3))),
            pltpu.SemaphoreType.DMA((3, max(CHUNKS, 3))),
        ],
        compiler_params=pltpu.CompilerParams(
            collective_id=mz, has_side_effects=True, vmem_limit_bytes=48 * 2**20
        ),
        name="codistill_step",
    )(partner, x, ids, w, s, gain, sgain)


def body(ngroups, tokens, token_ids, weight, stale_weight, gain, stale_gain, partner):
    branches = [functools.partial(step_for, mz) for mz in range(ngroups // NX)]
    gw, gt, loss = lax.switch(
        partner[0] // NX, branches,
        tokens[0], token_ids, weight[0], stale_weight[0], gain, stale_gain, partner,
    )
    return gw[None], gt[None], loss


def solution(mesh):
    return jax.shard_map(
        functools.partial(body, mesh.shape["group"]),
        mesh=mesh,
        in_specs=(
            P("group", "fsdp", None),
            P("group", "fsdp"),
            P("group", "fsdp", None),
            P("group", "fsdp", None),
            P("group", None),
            P("group", None),
            P(),
        ),
        out_specs=(P("group", "fsdp", None), P("group", "fsdp", None), P("group", "fsdp")),
        check_vma=False,
    )
```

time: 433 us -> 115 us (0.27)
  the two profiles are of different devices: /device:TPU:1 before, /device:TPU:4 now
where the time goes in v3:
time: 115 us; the launch traced here: 113 us
  Pallas kernels  108 us (94%)
  local copies, waits for them, and re-layouts  3.44 us (3%)
    pallas_call x1, Pallas kernels, step_for(): pl.pallas_call(functools.partial(step_kernel, mz), out_shape=(jax.ShapeDt...  108 us
    unnamed x11, local copies, waits for them, and re-layouts  3.44 us

profile of v3, /device:TPU:4, one launch (start us, length us, event | category | flops | bytes accessed | tf_op | source)
XLA Modules:
  0.0 113.0 jit_solution(5787320899139411441)
XLA Ops:
  0.6 0.0 copy-start.2
  0.6 0.6 copy-done.2
  1.4 0.0 copy-start.1
  1.4 0.0 copy-start
  1.5 0.0 copy-start.3
  1.5 0.6 copy-done.1
  2.1 0.0 copy-done
  2.1 0.0 copy-done.3
  2.1 108.7 %conditional.1 = (f32[1,128]{1,0:T(1,128)S(1)}, f32[1,144,1024]{2,1,0:T(8,128)S(1)}, bf16[1,128,2304]{2,1,0:T(8,128)(2,1)S(1)}) conditional(s32[]{:T(128)} %clamp.3, (s32[32]{0:T(128)S(1)}, bf16[128,2304]{1,0:T(8,128)(2,1)}, s32[1,128]{1,0:T(1,128)S(1)}, bf16[144,1024]{1,0:T(8,128)(2,1)}, ...), branch_computations={%region_0.1_spmd, %region_1.2_spmd, %region_2.3_spmd, %region_3.4_... | conditional | bytes 24 | solution.py:404
  2.1 108.4 %codistill_step.14 = (f32[144,1024]{1,0:T(8,128)S(1)}, bf16[128,2304]{1,0:T(8,128)(2,1)S(1)}, f32[1,128]{1,0:T(1,128)S(1)}) custom-call(s32[32]{0:T(128)S(1)} %get-tuple-element.198.partner_ref, bf16[128,2304]{1,0:T(8,128)(2,1)} %get-tuple-element.199.x_ref, s32[1,128]{1,0:T(1,128)S(1)} %get-tuple-element.200.ids_ref, ...), custom_call_target="tpu_custom_call" | custom-call | tf_op jit(solution)/shard_map/cond/branch_6_fun/codistill_step/pallas_call | solution.py:348
  110.9 0.8 copy.37
  111.7 0.8 copy.38
  112.5 0.5 copy.39
Async XLA Ops:
  0.6 0.7 copy-start.2
  1.4 0.7 copy-start.1
  1.4 0.7 copy-start
  1.5 0.7 copy-start.3

commit v4 on v3

--- a/solution.py
+++ b/solution.py
@@ -11,7 +11,7 @@
 NX = 4
 NY = 4
 CHUNKS = 4
-UNROLL = True
+UNROLL = False
 AHEAD = 1
 F32 = jnp.float32
 BF16 = jnp.bfloat16
@@ -199,7 +199,7 @@
     def column(j):
         gcols[j] = jnp.broadcast_to(sgx[3 + j], (128, chans)).T
 
-    each(2, column, UNROLL)
+    each(2, column)
 
     def stage_a(f):
         z_copy(0, f, wfull.at[f, block(far), :], wfull.at[f, block(far), :], twin).wait_recv()

time: 115 us -> 115 us (level)
  the two profiles are of different devices: /device:TPU:4 before, /device:TPU:32 now
where the time goes in v4:
time: 115 us
  Pallas kernels  110 us (96%)
  local copies, waits for them, and re-layouts  3.44 us (3%)
    pallas_call x1, Pallas kernels, step_for(): pl.pallas_call(functools.partial(step_kernel, mz), out_shape=(jax.ShapeDt...  110 us
    unnamed x11, local copies, waits for them, and re-layouts  3.44 us

profile of v4, /device:TPU:32, one launch (start us, length us, event | category | flops | bytes accessed | tf_op | source)
XLA Modules:
  0.0 114.7 jit_solution(4766153836212846600)
XLA Ops:
  0.6 0.0 copy-start.2
  0.6 0.6 copy-done.2
  1.4 0.0 copy-start.1
  1.4 0.0 copy-start
  1.5 0.0 copy-start.3
  1.5 0.6 copy-done.1
  2.1 0.0 copy-done
  2.1 0.0 copy-done.3
  2.1 110.4 %conditional.1 = (f32[1,128]{1,0:T(1,128)S(1)}, f32[1,144,1024]{2,1,0:T(8,128)S(1)}, bf16[1,128,2304]{2,1,0:T(8,128)(2,1)S(1)}) conditional(s32[]{:T(128)} %clamp.3, (s32[32]{0:T(128)S(1)}, bf16[128,2304]{1,0:T(8,128)(2,1)}, s32[1,128]{1,0:T(1,128)S(1)}, bf16[144,1024]{1,0:T(8,128)(2,1)}, ...), branch_computations={%region_0.1_spmd, %region_1.2_spmd, %region_2.3_spmd, %region_3.4_... | conditional | bytes 24 | solution.py:404
  2.1 110.4 %codistill_step.9 = (f32[144,1024]{1,0:T(8,128)S(1)}, bf16[128,2304]{1,0:T(8,128)(2,1)S(1)}, f32[1,128]{1,0:T(1,128)S(1)}) custom-call(s32[32]{0:T(128)S(1)} %get-tuple-element.148.partner_ref, bf16[128,2304]{1,0:T(8,128)(2,1)} %get-tuple-element.149.x_ref, s32[1,128]{1,0:T(1,128)S(1)} %get-tuple-element.150.ids_ref, ...), custom_call_target="tpu_custom_call" | custom-call | tf_op jit(solution)/shard_map/cond/branch_1_fun/codistill_step/pallas_call | solution.py:348
  112.5 0.8 copy.37
  113.3 0.8 copy.38
  114.2 0.5 copy.39
Async XLA Ops:
  0.6 0.7 copy-start.2
  1.4 0.7 copy-start.1
  1.4 0.7 copy-start
  1.5 0.7 copy-start.3
